TPU v7x, 32 devices: a whole 2x2x4 slice. The times are simulated.
32 devices in a mesh: head: 2 (over x), ctx: 16 (over z, y, core).
Axes of the slice: x: 2, y: 2, z: 4, core: 2. Of those that a mesh axis runs over, the one named last changes fastest.
Arguments:
- queries: bfloat16 [2048, 6144], P('ctx', 'head'), may hold values from -6 to 6
- key_rows: bfloat16 [2048, 1024], P('ctx', 'head'), may hold values from -6 to 6
- value_rows: bfloat16 [2048, 1024], P('ctx', 'head'), may hold values from -6 to 6
- out_grad: bfloat16 [2048, 6144], P('ctx', 'head'), may hold values from -24 to 24
- gate_logit: float32 [2048], P('ctx'), may hold values from -6 to 6
- tile_plan: int32 [16, 4, 16], replicated, may hold values from -1 to 15, as said below
- mask_kind: int32 [16, 4, 16], P('ctx'), may hold values from 0 to 1
Outputs:
- query_grad: bfloat16 [2048, 6144], P('ctx', 'head')
- key_grad: bfloat16 [2048, 1024], P('ctx', 'head')
- value_grad: bfloat16 [2048, 1024], P('ctx', 'head')
- gate_grad: float32 [2048], P('ctx')
Inputs may be any that keep to these rules, and one draw needn't show every extreme that they name: tile_plan[b, s, p] is a key tile of block p (of 8 rows) that block b reads in section s, or -1; it is -1 when p == b; the tiles that b reads from one p differ from section to section; in every section each block reads from between 4 and 8 blocks, and some block reads from exactly 8.
All inputs are finite; a program needn't handle non-finite values.
Results may differ from a plain program's by a relative error of at most 0.033.
Values may be sent and summed in bfloat16 or wider, within the bound.
A program may use at most 64 MiB of HBM per device.

v0:
```python
import math

import jax
import jax.numpy as jnp
from jax import lax
from jax.sharding import PartitionSpec as P

HD = 128
TILE = 8
SECTIONS = 4


big_negative = -1e30


def body(queries, key_rows, value_rows, out_grad, gate_logit, tile_plan, mask_kind):
    row_count = queries.shape[0]
    kv_count = key_rows.shape[1] // HD
    head_count = queries.shape[1] // HD
    group_size = head_count // kv_count
    kv_width = kv_count * HD
    tile_count = row_count // TILE
    peer_count = lax.axis_size("ctx")
    device = lax.axis_index("ctx")
    factor = 1.0 / math.sqrt(HD)
    row_index = jnp.arange(row_count, dtype=jnp.int32)
    late_rows = row_index >= row_count // 2
    tile_index = jnp.arange(tile_count, dtype=jnp.int32)
    plan_read = lax.dynamic_index_in_dim(tile_plan, device, 0, keepdims=False)
    plan_given = lax.dynamic_index_in_dim(tile_plan, device, 2, keepdims=False)
    slot_count = peer_count // 2
    slot_order = jnp.argsort((plan_read < 0).astype(jnp.int32), axis=1, stable=True)[:, :slot_count]
    slot_tiles = jnp.take_along_axis(plan_read, slot_order, axis=1)
    slot_kinds = jnp.take_along_axis(mask_kind[0], slot_order, axis=1)
    slot_seen = (slot_tiles >= 0)[None] & ((slot_kinds == 0)[None] | late_rows[:, None, None])
    joined = jnp.concatenate([key_rows, value_rows], axis=1).reshape(tile_count, TILE, 2 * kv_width)
    outgoing = jnp.where(
        (plan_given >= 0)[:, :, None, None],
        joined[jnp.maximum(plan_given, 0)],
        jnp.zeros((), jnp.bfloat16),
    )
    arrived = lax.all_to_all(outgoing, "ctx", split_axis=0, concat_axis=0, tiled=True)
    fetched = [arrived[:, section_index] for section_index in range(SECTIONS)]
    key_sets = [
        (
            key_rows.reshape(row_count, kv_count, HD),
            value_rows.reshape(row_count, kv_count, HD),
            row_index[:, None] >= row_index[None, :],
        )
    ]
    for section_index in range(SECTIONS):
        picked = jnp.take(fetched[section_index], slot_order[section_index], axis=0)
        picked = picked.reshape(slot_count * TILE, 2 * kv_width)
        visible = jnp.broadcast_to(
            slot_seen[:, section_index, :, None], (row_count, slot_count, TILE)
        ).reshape(row_count, slot_count * TILE)
        key_sets.append(
            (
                picked[:, :kv_width].reshape(-1, kv_count, HD),
                picked[:, kv_width:].reshape(-1, kv_count, HD),
                visible,
            )
        )
    query_heads = queries.reshape(row_count, kv_count, group_size, HD)
    grad_heads = out_grad.reshape(row_count, kv_count, group_size, HD)
    gate = jax.nn.sigmoid(gate_logit)
    d_attended = (gate[:, None, None, None] * grad_heads.astype(jnp.float32)).astype(jnp.bfloat16)
    running_top = jnp.full((kv_count, group_size, row_count), big_negative, jnp.float32)
    running_total = jnp.zeros((kv_count, group_size, row_count), jnp.float32)
    kept_scores = []
    for key_set, value_set, visible in key_sets:
        scores = (
            jnp.einsum("rcgd,kcd->cgrk", query_heads, key_set, preferred_element_type=jnp.float32)
            * factor
        )
        scores = jnp.where(visible[None, None], scores, big_negative)
        kept_scores.append(scores)
        new_top = jnp.maximum(running_top, jnp.max(scores, axis=-1))
        running_total = running_total * jnp.exp(running_top - new_top) + jnp.sum(
            jnp.exp(scores - new_top[..., None]), axis=-1
        )
        running_top = new_top
    log_total = running_top + jnp.log(running_total)
    attended_sum = jnp.zeros((row_count, kv_count, group_size, HD), jnp.float32)
    value_parts = []
    kept_probs = []
    for set_index in range(len(key_sets)):
        key_set, value_set, visible = key_sets[set_index]
        probs = jnp.exp(kept_scores[set_index] - log_total[..., None])
        kept_probs.append(probs)
        probs_low = probs.astype(jnp.bfloat16)
        attended_sum = attended_sum + jnp.einsum(
            "cgrk,kcd->rcgd", probs_low, value_set, preferred_element_type=jnp.float32
        )
        value_parts.append(
            jnp.einsum("cgrk,rcgd->kcd", probs_low, d_attended, preferred_element_type=jnp.float32)
        )
    attended = attended_sum.astype(jnp.bfloat16).astype(jnp.float32)
    gate_part = jnp.sum(grad_heads.astype(jnp.float32) * attended, axis=(1, 2, 3))
    gate_sum = lax.psum(gate_part, "head")
    gate_grad = gate * (1.0 - gate) * gate_sum
    delta = jnp.transpose(jnp.sum(d_attended.astype(jnp.float32) * attended, axis=-1), (1, 2, 0))
    query_sum = jnp.zeros((row_count, kv_count, group_size, HD), jnp.float32)
    grad_parts = []
    for set_index in range(len(key_sets)):
        key_set, value_set, visible = key_sets[set_index]
        probs = kept_probs[set_index]
        d_probs = jnp.einsum(
            "rcgd,kcd->cgrk", d_attended, value_set, preferred_element_type=jnp.float32
        )
        d_scores = (probs * (d_probs - delta[..., None])).astype(jnp.bfloat16)
        query_sum = query_sum + jnp.einsum(
            "cgrk,kcd->rcgd", d_scores, key_set, preferred_element_type=jnp.float32
        )
        key_part = (
            jnp.einsum("cgrk,rcgd->kcd", d_scores, query_heads, preferred_element_type=jnp.float32)
            * factor
        )
        both_parts = jnp.concatenate(
            [key_part.reshape(-1, kv_width), value_parts[set_index].reshape(-1, kv_width)], axis=1
        )
        grad_parts.append(both_parts)
    returns = []
    for section_index in range(SECTIONS):
        slot_part = grad_parts[section_index + 1].reshape(slot_count, TILE, 2 * kv_width)
        placing = (
            slot_order[section_index][:, None] == jnp.arange(peer_count, dtype=jnp.int32)[None, :]
        ).astype(jnp.float32)
        returns.append(
            jnp.einsum("wn,wrc->nrc", placing, slot_part, precision=lax.Precision.HIGHEST)
        )
    returned_all = lax.all_to_all(
        jnp.stack(returns, axis=1).astype(jnp.bfloat16),
        "ctx",
        split_axis=0,
        concat_axis=0,
        tiled=True,
    ).astype(jnp.float32)
    owners = (plan_given[:, :, None] == tile_index[None, None, :]).astype(jnp.float32)
    owner_sum = jnp.einsum("nst,nsrc->trc", owners, returned_all, precision=lax.Precision.HIGHEST)
    local_sum = grad_parts[0] + owner_sum.reshape(row_count, 2 * kv_width)
    query_grad = (query_sum * factor).reshape(row_count, head_count * HD).astype(jnp.bfloat16)
    key_grad = local_sum[:, :kv_width].astype(jnp.bfloat16)
    value_grad = local_sum[:, kv_width:].astype(jnp.bfloat16)
    return (query_grad, key_grad, value_grad, gate_grad)


def solution(mesh):
    placed = (
        P("ctx", "head"),
        P("ctx", "head"),
        P("ctx", "head"),
        P("ctx", "head"),
        P("ctx"),
        P(),
        P("ctx", None, None),
    )
    return jax.shard_map(
        body,
        mesh=mesh,
        in_specs=placed,
        out_specs=(P("ctx", "head"), P("ctx", "head"), P("ctx", "head"), P("ctx")),
        check_vma=False,
    )
```

profile of v0, /device:TPU:0, one launch (start us, length us, event | category | flops | bytes accessed | tf_op | source)
XLA Modules:
  0.0 136.9 jit_solution(9038497763340260772)
XLA Ops:
  0.6 1.2 maximum_reduce_fusion
  3.8 1.1 broadcast_select_fusion
  4.9 7.5 %all-to-all-start = ((bf16[16,4,8,1024]{3,2,1,0:T(8,128)(2,1)}), bf16[16,4,8,1024]{3,2,1,0:T(8,128)(2,1)S(1)}, u32[]{:S(2)}, u32[]{:S(2)}) async-start(bf16[16,4,8,1024]{3,2,1,0:T(8,128)(2,1)} %broadcast_select_fusion), calls=%async_computation | async-start | bytes 2097152 | tf_op jit(solution)/shard_map/all_to_all | solution.py:42
  22.0 1.4 %copy.292 = f32[128,3072]{0,1:T(8,128)} copy(bf16[128,3072]{1,0:T(8,128)(2,1)S(1)} %copy-done.10) | data formatting | bytes 2359296 | tf_op jit(solution)/shard_map/convert_element_type | solution.py:67
  26.4 1.7 %fusion.126 = (f32[4,6,128]{2,1,0:T(8,128)}, f32[4,6,128,128]{2,3,1,0:T(8,128)S(1)}) fusion(bf16[128,4,128,1]{0,2,3,1:T(8,128)(2,1)S(1)} %copy.368, bf16[128,4,6,128]{0,3,2,1:T(8,128)(2,1)S(1)} %bitcast.297, pred[128,128]{0,1:T(8,128)(4,1)} %iota_compare_fusion), kind=kOutput, calls=%fused_computation.222 | convolution fusion | flops 101839872 | bytes 2519040 | tf_op jit(solution)/shard_map/rcgd,kcd->cgrk/dot_general | solution.py:73
  28.2 7.2 %all-to-all-done = bf16[16,4,8,1024]{3,2,1,0:T(8,128)(2,1)S(1)} async-done(((bf16[16,4,8,1024]{3,2,1,0:T(8,128)(2,1)}), bf16[16,4,8,1024]{3,2,1,0:T(8,128)(2,1)S(1)}, u32[]{:S(2)}, u32[]{:S(2)}) %all-to-all-start) | async-done | bytes 1048608 | tf_op jit(solution)/shard_map/all_to_all | solution.py:42
  36.4 1.7 %gather_fusion.3 = bf16[8,8,1024]{2,1,0:T(8,128)(2,1)S(1)} fusion(bf16[16,8,1024]{2,1,0:T(8,128)(2,1)} %get-tuple-element.45, s32[1024]{0:T(1024)} %pad_clamp_fusion.3), kind=kCustom, calls=%fused_computation.1.clone | custom fusion | bytes 262176 | tf_op jit(solution)/shard_map/jit(_take)/gather | solution.py:52
  38.9 1.6 %gather_fusion.6 = bf16[8,8,1024]{2,1,0:T(8,128)(2,1)S(1)} fusion(bf16[16,8,1024]{2,1,0:T(8,128)(2,1)} %get-tuple-element.46, s32[1024]{0:T(1024)} %pad_clamp_fusion), kind=kCustom, calls=%fused_computation.5.clone | custom fusion | bytes 262176 | tf_op jit(solution)/shard_map/jit(_take)/gather | solution.py:52
  50.8 1.1 convolution_bitcast_fusion.10
  51.8 1.0 fusion.25
  52.9 1.1 fusion.26
  55.0 1.0 fusion.27
  56.0 1.1 convolution_bitcast_fusion.6
  57.1 1.0 fusion.24
  58.1 1.4 %fusion.6 = bf16[4,6,128,128]{2,3,1,0:T(8,128)(2,1)} fusion(bf16[128,4,128,1]{0,2,3,1:T(8,128)(2,1)S(1)} %copy-done.7, bf16[128,4,6,128]{0,3,2,1:T(8,128)(2,1)S(1)} %get-tuple-element.34, f32[4,6,128,128]{2,3,1,0:T(8,128)S(1)} %get-tuple-element.73, f32[4,6,128]{2,1,0:T(8,128)S(1)} %bitcast.316, f32[4,6,128]{2,1,0:T(8,128)S(1)} %log_add_fusion), kind=kOutput, calls=%fused_computation.24 | convolution fusion | flops 102236160 | bytes 3301376 | tf_op jit(solution)/shard_map/rcgd,kcd->cgrk/dot_general | solution.py:108
  61.3 1.4 %fusion.36 = f32[64,4,128]{2,0,1:T(8,128)S(1)} fusion(bf16[4,6,128,64]{2,3,1,0:T(8,128)(2,1)} %fusion.25, bf16[128,4,6,128]{0,3,2,1:T(8,128)(2,1)S(1)} %bitcast.302), kind=kOutput, calls=%fused_computation.76 | convolution fusion | flops 50364416 | bytes 1310720 | tf_op jit(solution)/shard_map/cgrk,rcgd->kcd/dot_general | solution.py:116
  63.4 1.6 %concatenate.46 = f32[8,8,512]{2,1,0:T(8,128)} reshape(f32[64,4,128]{2,1,0:T(4,128)} %copy.333) | data formatting | bytes 262144 | tf_op jit(solution)/shard_map/concatenate | solution.py:119
  65.0 1.6 %copy.336 = f32[8,8,512]{2,0,1:T(8,128)} copy(f32[8,8,512]{2,1,0:T(8,128)} %concatenate.46) | data formatting | bytes 262144 | tf_op jit(solution)/shard_map/concatenate | solution.py:119
  66.7 1.6 %copy.329 = f32[64,4,128]{2,1,0:T(4,128)} copy(f32[64,4,128]{2,0,1:T(8,128)} %convolution_bitcast_fusion.10) | data formatting | bytes 262144 | tf_op jit(solution)/shard_map/cgrk,rcgd->kcd/transpose | solution.py:96
  68.3 1.6 %concatenate.44 = f32[8,8,512]{2,1,0:T(8,128)} reshape(f32[64,4,128]{2,1,0:T(4,128)} %copy.329) | data formatting | bytes 262144 | tf_op jit(solution)/shard_map/concatenate | solution.py:119
  69.9 1.6 %copy.331 = f32[8,8,512]{2,0,1:T(8,128)} copy(f32[8,8,512]{2,1,0:T(8,128)} %concatenate.44) | data formatting | bytes 262144 | tf_op jit(solution)/shard_map/concatenate | solution.py:119
  71.6 1.4 %fusion.38 = f32[64,4,128]{2,0,1:T(8,128)S(1)} fusion(bf16[4,6,128,64]{2,3,1,0:T(8,128)(2,1)} %fusion.26, bf16[128,4,6,128]{0,3,2,1:T(8,128)(2,1)S(1)} %bitcast.303), kind=kOutput, calls=%fused_computation.80 | convolution fusion | flops 50364416 | bytes 1310720 | tf_op jit(solution)/shard_map/cgrk,rcgd->kcd/dot_general | solution.py:116
  73.7 1.6 %concatenate.43 = f32[8,8,512]{2,1,0:T(8,128)} reshape(f32[64,4,128]{2,1,0:T(4,128)} %copy.327) | data formatting | bytes 262144 | tf_op jit(solution)/shard_map/concatenate | solution.py:119
  75.3 1.6 %copy.330 = f32[8,8,512]{2,0,1:T(8,128)} copy(f32[8,8,512]{2,1,0:T(8,128)} %concatenate.43) | data formatting | bytes 262144 | tf_op jit(solution)/shard_map/concatenate | solution.py:119
  76.9 1.6 %copy.323 = f32[64,4,128]{2,1,0:T(4,128)} copy(f32[64,4,128]{2,0,1:T(8,128)} %convolution_bitcast_fusion.12) | data formatting | bytes 262144 | tf_op jit(solution)/shard_map/cgrk,rcgd->kcd/transpose | solution.py:96
  78.6 1.6 %concatenate.41 = f32[8,8,512]{2,1,0:T(8,128)} reshape(f32[64,4,128]{2,1,0:T(4,128)} %copy.323) | data formatting | bytes 262144 | tf_op jit(solution)/shard_map/concatenate | solution.py:119
  80.2 1.6 %copy.325 = f32[8,8,512]{2,0,1:T(8,128)} copy(f32[8,8,512]{2,1,0:T(8,128)} %concatenate.41) | data formatting | bytes 262144 | tf_op jit(solution)/shard_map/concatenate | solution.py:119
  81.8 1.4 %fusion.40 = f32[64,4,128]{2,0,1:T(8,128)S(1)} fusion(bf16[4,6,128,64]{2,3,1,0:T(8,128)(2,1)} %fusion.27, bf16[128,4,6,128]{0,3,2,1:T(8,128)(2,1)S(1)} %bitcast.304), kind=kOutput, calls=%fused_computation.84 | convolution fusion | flops 50364416 | bytes 1310720 | tf_op jit(solution)/shard_map/cgrk,rcgd->kcd/dot_general | solution.py:116
  83.9 1.6 %concatenate.40 = f32[8,8,512]{2,1,0:T(8,128)} reshape(f32[64,4,128]{2,1,0:T(4,128)} %copy.321) | data formatting | bytes 262144 | tf_op jit(solution)/shard_map/concatenate | solution.py:119
  85.6 1.6 %copy.324 = f32[8,8,512]{2,0,1:T(8,128)} copy(f32[8,8,512]{2,1,0:T(8,128)} %concatenate.40) | data formatting | bytes 262144 | tf_op jit(solution)/shard_map/concatenate | solution.py:119
  87.2 1.6 %copy.341 = f32[64,4,128]{2,1,0:T(4,128)} copy(f32[64,4,128]{2,0,1:T(8,128)} %convolution_bitcast_fusion.6) | data formatting | bytes 262144 | tf_op jit(solution)/shard_map/cgrk,rcgd->kcd/transpose | solution.py:96
  88.8 1.6 %concatenate.50 = f32[8,8,512]{2,1,0:T(8,128)} reshape(f32[64,4,128]{2,1,0:T(4,128)} %copy.341) | data formatting | bytes 262144 | tf_op jit(solution)/shard_map/concatenate | solution.py:119
  90.5 1.6 %copy.343 = f32[8,8,512]{2,0,1:T(8,128)} copy(f32[8,8,512]{2,1,0:T(8,128)} %concatenate.50) | data formatting | bytes 262144 | tf_op jit(solution)/shard_map/concatenate | solution.py:119
  92.1 1.4 %fusion.34 = f32[64,4,128]{2,0,1:T(8,128)S(1)} fusion(bf16[4,6,128,64]{2,3,1,0:T(8,128)(2,1)} %fusion.24, bf16[128,4,6,128]{0,3,2,1:T(8,128)(2,1)S(1)} %bitcast.305), kind=kOutput, calls=%fused_computation.72 | convolution fusion | flops 50364416 | bytes 1310720 | tf_op jit(solution)/shard_map/cgrk,rcgd->kcd/dot_general | solution.py:116
  94.2 1.6 %concatenate.49 = f32[8,8,512]{2,1,0:T(8,128)} reshape(f32[64,4,128]{2,1,0:T(4,128)} %copy.339) | data formatting | bytes 262144 | tf_op jit(solution)/shard_map/concatenate | solution.py:119
  96.9 1.4 %fusion.30 = bf16[16,1,8,1024]{3,0,2,1:T(8,128)(2,1)S(1)} fusion(f32[8,8,512]{2,0,1:T(8,128)S(1)} %copy.337, f32[8,8,512]{2,0,1:T(8,128)} %copy.336, s32[8]{0:T(128)S(1)} %copy-done.43), kind=kOutput, calls=%fused_computation.65 | convolution fusion | flops 12779648 | bytes 524320 | tf_op jit(solution)/shard_map/wn,wrc->nrc/dot_general | solution.py:130
  98.3 1.5 %fusion.29 = bf16[16,1,8,1024]{3,0,2,1:T(8,128)(2,1)S(1)} fusion(f32[8,8,512]{2,0,1:T(8,128)} %copy.331, f32[8,8,512]{2,0,1:T(8,128)} %copy.330, s32[8]{0:T(128)S(1)} %copy-done.40), kind=kOutput, calls=%fused_computation.64 | convolution fusion | flops 12779648 | bytes 524320 | tf_op jit(solution)/shard_map/wn,wrc->nrc/dot_general | solution.py:130
  99.8 1.5 %fusion.28 = bf16[16,1,8,1024]{3,0,2,1:T(8,128)(2,1)S(1)} fusion(f32[8,8,512]{2,0,1:T(8,128)} %copy.325, f32[8,8,512]{2,0,1:T(8,128)} %copy.324, s32[8]{0:T(128)S(1)} %copy-done.37), kind=kOutput, calls=%fused_computation.63 | convolution fusion | flops 12779648 | bytes 524320 | tf_op jit(solution)/shard_map/wn,wrc->nrc/dot_general | solution.py:130
  101.9 1.6 %copy.344 = bf16[16,4,8,1024]{3,2,1,0:T(8,128)(2,1)} copy(bf16[16,4,8,1024]{3,0,2,1:T(8,128)(2,1)S(1)} %pad_maximum_fusion) | data formatting | bytes 2097152 | tf_op jit(solution)/shard_map/stack | solution.py:133
  103.4 6.9 %all-to-all-start.1 = ((bf16[16,4,8,1024]{3,2,1,0:T(8,128)(2,1)}), bf16[16,4,8,1024]{3,2,1,0:T(8,128)(2,1)}, u32[]{:S(2)}, u32[]{:S(2)}) async-start(bf16[16,4,8,1024]{3,2,1,0:T(8,128)(2,1)} %copy.344), calls=%async_computation.1 | async-start | bytes 2097152 | tf_op jit(solution)/shard_map/all_to_all | solution.py:132
  110.4 2.2 %fusion.32 = f32[4,128,128]{1,2,0:T(8,128)} fusion(bf16[4,6,128,128]{2,3,1,0:T(8,128)(2,1)} %fusion.6, bf16[128,4,6,128]{0,3,2,1:T(8,128)(2,1)S(1)} %bitcast.306), kind=kOutput, calls=%fused_computation.68 | convolution fusion | flops 100728832 | bytes 1835008 | tf_op jit(solution)/shard_map/cgrk,rcgd->kcd/dot_general | solution.py:116
  112.6 1.8 %copy.318 = f32[128,512]{1,0:T(8,128)} copy(f32[128,512]{0,1:T(8,128)} %bitcast.311) | data formatting | bytes 524288 | tf_op jit(solution)/shard_map/reshape | solution.py:120
  114.4 1.1 fusion.59
  115.4 1.1 copy.319
  119.4 1.2 copy.347
  120.6 4.9 %psum.7 = f32[128]{0:T(128)S(1)} all-reduce(f32[128]{0:T(128)S(1)} %get-tuple-element.28), channel_id=1, replica_groups=mesh['head'=2,'ctx'=16] {'head'}, use_global_device_ids=true, to_apply=%region_13.16 | all-reduce | flops 128 | bytes 1024 | tf_op jit(solution)/shard_map/psum | solution.py:100
  126.0 7.3 %all-to-all-done.1 = bf16[16,4,8,1024]{3,2,1,0:T(8,128)(2,1)} async-done(((bf16[16,4,8,1024]{3,2,1,0:T(8,128)(2,1)}), bf16[16,4,8,1024]{3,2,1,0:T(8,128)(2,1)}, u32[]{:S(2)}, u32[]{:S(2)}) %all-to-all-start.1) | async-done | bytes 1048608 | tf_op jit(solution)/shard_map/all_to_all | solution.py:132
  133.4 2.4 %convolution_bitcast_fusion.4 = f32[16,8,1024]{2,0,1:T(8,128)S(1)} fusion(bf16[16,4,8,1024]{3,2,1,0:T(8,128)(2,1)} %all-to-all-done.1, s32[16,4]{0,1:T(4,128)S(1)} %bitcast.335), kind=kOutput, calls=%fused_computation.58 | convolution fusion | flops 16778240 | bytes 1573120 | tf_op jit(solution)/shard_map/nst,nsrc->trc/dot_general | solution.py:140
  (199 shorter events, 37.8 us)
Async XLA Ops:
  0.6 17.6 %copy-start = (s32[1,4,16]{2,1,0:T(4,128)S(1)}, s32[1,4,16]{2,1,0:T(4,128)}, u32[]{:S(2)}) copy-start(s32[1,4,16]{2,1,0:T(4,128)} %param.17) | copy-start | bytes 772
  4.9 9.9 %copy-start.28 = (bf16[128,512]{1,0:T(8,128)(2,1)S(1)}, bf16[128,512]{1,0:T(8,128)(2,1)}, u32[]{:S(2)}) copy-start(bf16[128,512]{1,0:T(8,128)(2,1)} %param.12) | copy-start | bytes 393220
  4.9 9.9 %copy-start.29 = (bf16[128,512]{1,0:T(8,128)(2,1)S(1)}, bf16[128,512]{1,0:T(8,128)(2,1)}, u32[]{:S(2)}) copy-start(bf16[128,512]{1,0:T(8,128)(2,1)} %param.13) | copy-start | bytes 393220
  4.9 30.5 %all-to-all-start = ((bf16[16,4,8,1024]{3,2,1,0:T(8,128)(2,1)}), bf16[16,4,8,1024]{3,2,1,0:T(8,128)(2,1)S(1)}, u32[]{:S(2)}, u32[]{:S(2)}) async-start(bf16[16,4,8,1024]{3,2,1,0:T(8,128)(2,1)} %broadcast_select_fusion), calls=%async_computation | async-start | bytes 2097152 | tf_op jit(solution)/shard_map/all_to_all | solution.py:42
  14.1 4.8 %copy-start.38 = (s32[8]{0:T(128)}, s32[8]{0:T(128)S(1)}, u32[]{:S(2)}) copy-start(s32[8]{0:T(128)S(1)} %get-tuple-element.32) | copy-start | bytes 100
  14.1 4.8 %copy-start.41 = (s32[8]{0:T(128)}, s32[8]{0:T(128)S(1)}, u32[]{:S(2)}) copy-start(s32[8]{0:T(128)S(1)} %get-tuple-element.30) | copy-start | bytes 100
  14.2 9.8 %copy-start.34 = (s32[8]{0:T(128)}, s32[8]{0:T(128)S(1)}, u32[]{:S(2)}) copy-start(s32[8]{0:T(128)S(1)} %get-tuple-element.31) | copy-start | bytes 100
  14.2 10.3 %copy-start.36 = (s32[8]{0:T(128)}, s32[8]{0:T(128)S(1)}, u32[]{:S(2)}) copy-start(s32[8]{0:T(128)S(1)} %get-tuple-element.33) | copy-start | bytes 100
  18.2 3.3 %copy-start.9 = (bf16[128,3072]{1,0:T(8,128)(2,1)S(1)}, bf16[128,3072]{1,0:T(8,128)(2,1)}, u32[]{:S(2)}) copy-start(bf16[128,3072]{1,0:T(8,128)(2,1)} %param.11) | copy-start | bytes 2359300
  19.0 2.9 %copy-start.10 = (bf16[128,3072]{1,0:T(8,128)(2,1)S(1)}, bf16[128,3072]{1,0:T(8,128)(2,1)}, u32[]{:S(2)}) copy-start(bf16[128,3072]{1,0:T(8,128)(2,1)} %param.14) | copy-start | bytes 2359300
  21.9 1.5 %copy-start.47 = (f32[128]{0:T(128)S(1)}, f32[128]{0:T(128)}, u32[]{:S(2)}) copy-start(f32[128]{0:T(128)} %param.15) | copy-start | bytes 1540
  21.9 2.0 %copy-start.42 = (s32[8]{0:T(128)S(1)}, s32[8]{0:T(128)}, u32[]{:S(2)}) copy-start(s32[8]{0:T(128)} %copy-done.41) | copy-start | bytes 100
  22.0 2.5 %copy-start.39 = (s32[8]{0:T(128)S(1)}, s32[8]{0:T(128)}, u32[]{:S(2)}) copy-start(s32[8]{0:T(128)} %copy-done.38) | copy-start | bytes 100
  22.0 3.1 %copy-start.45 = (pred[4,8]{1,0:T(4,128)(4,1)S(1)}, pred[4,8]{1,0:T(4,128)(4,1)}, u32[]{:S(2)}) copy-start(pred[4,8]{1,0:T(4,128)(4,1)} %copy.278) | copy-start | bytes 100
  22.0 3.1 %copy-start.46 = (pred[4,8]{1,0:T(4,128)(4,1)S(1)}, pred[4,8]{1,0:T(4,128)(4,1)}, u32[]{:S(2)}) copy-start(pred[4,8]{1,0:T(4,128)(4,1)} %copy.281) | copy-start | bytes 100
  36.4 5.0 %copy-start.26 = (bf16[16,8,1024]{2,1,0:T(8,128)(2,1)S(1)}, bf16[16,8,1024]{2,1,0:T(8,128)(2,1)}, u32[]{:S(2)}) copy-start(bf16[16,8,1024]{2,1,0:T(8,128)(2,1)} %get-tuple-element.47) | copy-start | bytes 786436
  36.4 6.5 %copy-start.25 = (bf16[16,8,1024]{2,1,0:T(8,128)(2,1)S(1)}, bf16[16,8,1024]{2,1,0:T(8,128)(2,1)}, u32[]{:S(2)}) copy-start(bf16[16,8,1024]{2,1,0:T(8,128)(2,1)} %get-tuple-element.48) | copy-start | bytes 786436
  38.9 9.2 %copy-start.17 = (bf16[64,4,128]{2,1,0:T(4,128)(2,1)}, bf16[64,4,128]{2,1,0:T(4,128)(2,1)S(1)}, u32[]{:S(2)}) copy-start(bf16[64,4,128]{2,1,0:T(4,128)(2,1)S(1)} %reshape.237) | copy-start | bytes 196612
  38.9 5.5 %copy-start.33 = (pred[128,64]{0,1:T(8,128)(4,1)S(1)}, pred[128,64]{0,1:T(8,128)(4,1)}, u32[]{:S(2)}) copy-start(pred[128,64]{0,1:T(8,128)(4,1)} %get-tuple-element.82) | copy-start | bytes 24580
  41.3 6.4 %copy-start.19 = (bf16[64,4,128]{2,1,0:T(4,128)(2,1)}, bf16[64,4,128]{2,1,0:T(4,128)(2,1)S(1)}, u32[]{:S(2)}) copy-start(bf16[64,4,128]{2,1,0:T(4,128)(2,1)S(1)} %reshape.240) | copy-start | bytes 196612
  41.3 3.3 %copy-start.11 = (bf16[64,4,128]{2,1,0:T(4,128)(2,1)}, bf16[64,4,128]{2,1,0:T(4,128)(2,1)S(1)}, u32[]{:S(2)}) copy-start(bf16[64,4,128]{2,1,0:T(4,128)(2,1)S(1)} %reshape.235) | copy-start | bytes 196612
  42.7 1.9 %copy-start.32 = (pred[128,64]{0,1:T(8,128)(4,1)S(1)}, pred[128,64]{0,1:T(8,128)(4,1)}, u32[]{:S(2)}) copy-start(pred[128,64]{0,1:T(8,128)(4,1)} %get-tuple-element.83) | copy-start | bytes 24580
  42.8 4.4 %copy-start.21 = (bf16[64,4,128]{2,1,0:T(4,128)(2,1)}, bf16[64,4,128]{2,1,0:T(4,128)(2,1)S(1)}, u32[]{:S(2)}) copy-start(bf16[64,4,128]{2,1,0:T(4,128)(2,1)S(1)} %reshape.239) | copy-start | bytes 196612
  42.8 2.1 %copy-start.13 = (bf16[64,4,128]{2,1,0:T(4,128)(2,1)}, bf16[64,4,128]{2,1,0:T(4,128)(2,1)S(1)}, u32[]{:S(2)}) copy-start(bf16[64,4,128]{2,1,0:T(4,128)(2,1)S(1)} %reshape.233) | copy-start | bytes 196612
  44.3 2.5 %copy-start.23 = (bf16[64,4,128]{2,1,0:T(4,128)(2,1)}, bf16[64,4,128]{2,1,0:T(4,128)(2,1)S(1)}, u32[]{:S(2)}) copy-start(bf16[64,4,128]{2,1,0:T(4,128)(2,1)S(1)} %reshape.238) | copy-start | bytes 196612
  48.1 1.4 %copy-start.2 = (f32[128,3072]{0,1:T(8,128)S(1)}, f32[128,3072]{0,1:T(8,128)}, u32[]{:S(2)}) copy-start(f32[128,3072]{0,1:T(8,128)} %copy.292) | copy-start | bytes 4718596
  48.1 1.4 %copy-start.7 = (bf16[128,4,128,1]{0,2,3,1:T(8,128)(2,1)S(1)}, bf16[128,4,128,1]{0,2,3,1:T(8,128)(2,1)}, u32[]{:S(2)}) copy-start(bf16[128,4,128,1]{0,2,3,1:T(8,128)(2,1)} %copy.362) | copy-start | bytes 393220
  48.1 1.4 %copy-start.44 = (f32[128]{0:T(128)S(1)}, f32[128]{0:T(128)}, u32[]{:S(2)}) copy-start(f32[128]{0:T(128)} %add_divide_fusion) | copy-start | bytes 1540
  50.4 1.5 %copy-start.22 = (bf16[64,4,128]{2,1,0:T(4,128)(2,1)S(1)}, bf16[64,4,128]{2,1,0:T(4,128)(2,1)}, u32[]{:S(2)}) copy-start(bf16[64,4,128]{2,1,0:T(4,128)(2,1)} %copy-done.21) | copy-start | bytes 196612
  50.8 2.1 %copy-start.24 = (bf16[64,4,128]{2,1,0:T(4,128)(2,1)S(1)}, bf16[64,4,128]{2,1,0:T(4,128)(2,1)}, u32[]{:S(2)}) copy-start(bf16[64,4,128]{2,1,0:T(4,128)(2,1)} %copy-done.23) | copy-start | bytes 196612
  52.9 2.1 %copy-start.18 = (bf16[64,4,128]{2,1,0:T(4,128)(2,1)S(1)}, bf16[64,4,128]{2,1,0:T(4,128)(2,1)}, u32[]{:S(2)}) copy-start(bf16[64,4,128]{2,1,0:T(4,128)(2,1)} %copy-done.17) | copy-start | bytes 196612
  55.0 2.1 %copy-start.20 = (bf16[64,4,128]{2,1,0:T(4,128)(2,1)S(1)}, bf16[64,4,128]{2,1,0:T(4,128)(2,1)}, u32[]{:S(2)}) copy-start(bf16[64,4,128]{2,1,0:T(4,128)(2,1)} %copy-done.19) | copy-start | bytes 196612
  85.6 11.3 %copy-start.43 = (s32[8]{0:T(128)S(1)}, s32[8]{0:T(128)}, u32[]{:S(2)}) copy-start(s32[8]{0:T(128)} %copy-done.41) | copy-start | bytes 100
  88.8 9.4 %copy-start.40 = (s32[8]{0:T(128)S(1)}, s32[8]{0:T(128)}, u32[]{:S(2)}) copy-start(s32[8]{0:T(128)} %copy-done.38) | copy-start | bytes 100
  92.1 7.7 %copy-start.37 = (s32[8]{0:T(128)S(1)}, s32[8]{0:T(128)}, u32[]{:S(2)}) copy-start(s32[8]{0:T(128)} %copy-done.36) | copy-start | bytes 100
  92.1 9.1 %copy-start.35 = (s32[8]{0:T(128)S(1)}, s32[8]{0:T(128)}, u32[]{:S(2)}) copy-start(s32[8]{0:T(128)} %copy-done.34) | copy-start | bytes 100
  95.8 5.4 %copy-start.27 = (f32[8,8,512]{2,0,1:T(8,128)S(1)}, f32[8,8,512]{2,0,1:T(8,128)}, u32[]{:S(2)}) copy-start(f32[8,8,512]{2,0,1:T(8,128)} %copy.343) | copy-start | bytes 393220
  103.4 29.9 %all-to-all-start.1 = ((bf16[16,4,8,1024]{3,2,1,0:T(8,128)(2,1)}), bf16[16,4,8,1024]{3,2,1,0:T(8,128)(2,1)}, u32[]{:S(2)}, u32[]{:S(2)}) async-start(bf16[16,4,8,1024]{3,2,1,0:T(8,128)(2,1)} %copy.344), calls=%async_computation.1 | async-start | bytes 2097152 | tf_op jit(solution)/shard_map/all_to_all | solution.py:132
  114.4 2.2 %copy-start.6 = (bf16[4,6,128,64]{2,3,1,0:T(8,128)(2,1)S(1)}, bf16[4,6,128,64]{2,3,1,0:T(8,128)(2,1)}, u32[]{:S(2)}) copy-start(bf16[4,6,128,64]{2,3,1,0:T(8,128)(2,1)} %fusion.24) | copy-start | bytes 1179652
  114.4 2.2 %copy-start.12 = (bf16[64,4,128]{2,1,0:T(4,128)(2,1)S(1)}, bf16[64,4,128]{2,1,0:T(4,128)(2,1)}, u32[]{:S(2)}) copy-start(bf16[64,4,128]{2,1,0:T(4,128)(2,1)} %copy-done.11) | copy-start | bytes 196612
  115.4 1.6 %copy-start.5 = (bf16[4,6,128,64]{2,3,1,0:T(8,128)(2,1)S(1)}, bf16[4,6,128,64]{2,3,1,0:T(8,128)(2,1)}, u32[]{:S(2)}) copy-start(bf16[4,6,128,64]{2,3,1,0:T(8,128)(2,1)} %fusion.27) | copy-start | bytes 1179652
  116.6 1.0 copy-start.4
  116.6 1.0 copy-start.16
  117.0 1.0 copy-start.3
  117.1 1.0 copy-start.14
  117.6 1.2 copy-start.1
  119.4 6.1 %copy-start.48 = (f32[128]{0:T(128)S(1)}, f32[128]{0:T(128)}, u32[]{:S(2)}) copy-start(f32[128]{0:T(128)} %param.15) | copy-start | bytes 1540
  119.4 16.4 %copy-start.8 = (f32[128,512]{1,0:T(8,128)S(1)}, f32[128,512]{1,0:T(8,128)}, u32[]{:S(2)}) copy-start(f32[128,512]{1,0:T(8,128)} %copy.318) | copy-start | bytes 786436
  (3 other events, 2.1 us)
where the time goes:
time: 139 us; the launch traced here: 137 us
  local copies, waits for them, and re-layouts  54.5 us (39%)
  matrix products  32.7 us (24%)
  waiting for transfers between devices  14.5 us (10%)
  starting transfers between devices  14.4 us (10%)
  other arithmetic  14.3 us (10%)
  blocking collectives  4.91 us (4%)
  between operations  1.48 us (1%)
    concatenate x16, local copies, waits for them, and re-layouts, body(): jnp.concatenate([key_part.reshape(-1, kv_width), value_parts[set_index].r...  23.8 us
    dot_general x5, matrix products, body(): jnp.einsum('cgrk,rcgd->kcd', d_scores, query_heads, preferred_element_typ...  7.76 us
    all_to_all x1, starting transfers between devices, body(): lax.all_to_all(outgoing, 'ctx', split_axis=0, concat_axis=0, tiled=True)  7.52 us
    all_to_all x1, waiting for transfers between devices, body(): lax.all_to_all(jnp.stack(returns, axis=1).astype(jnp.bfloat16), 'ctx', sp...  7.3 us
    all_to_all x1, waiting for transfers between devices, body(): lax.all_to_all(outgoing, 'ctx', split_axis=0, concat_axis=0, tiled=True)  7.22 us
    all_to_all x1, starting transfers between devices, body(): lax.all_to_all(jnp.stack(returns, axis=1).astype(jnp.bfloat16), 'ctx', sp...  6.92 us
    dot_general x5, matrix products, body(): jnp.einsum('rcgd,kcd->cgrk', d_attended, value_set, preferred_element_typ...  5.57 us
    transpose x4, local copies, waits for them, and re-layouts, body(): jnp.einsum('cgrk,rcgd->kcd', probs_low, d_attended, preferred_element_typ...  5.02 us
  transfers between devices with their start and end apart: 2, of which 2 were waited for; matrix products, arithmetic and copies ran while one was open for 19% of the time, Pallas kernels for 0%

commit v1 on v0

v1 whole, which is shorter than its diff:
```python
import functools
import math

import jax
import jax.numpy as jnp
from jax import lax
from jax.experimental import pallas as pl
from jax.experimental.pallas import tpu as pltpu
from jax.sharding import PartitionSpec as P

HD = 128
TILE = 8
LINE = False

NEG = -1e30


def contract(a, b, dim_a, dim_b):
    return lax.dot_general(
        a, b, (((dim_a,), (dim_b,)), ((), ())), preferred_element_type=jnp.float32
    )


def kernel(
    peers,
    line_size,
    head_peers,
    q_ref,
    k_ref,
    v_ref,
    og_ref,
    gate_row_ref,
    gate_col_ref,
    plan_ref,
    kind_ref,
    dq_ref,
    dk_ref,
    dv_ref,
    dgate_ref,
    pick,
    bias,
    line,
    x_out,
    x_in,
    g_out,
    g_in,
    own_grad,
    q_rows,
    q_cols,
    da_rows,
    da_cols,
    og_cols,
    kv_all,
    probs_kept,
    scores_kept,
    gate_parts,
    r_send_buf,
    r_recv_buf,
    x_send,
    x_recv,
    g_send,
    g_recv,
    l_send,
    l_recv,
    r_send,
    r_recv,
    p_send,
    p_recv,
):
    rows = q_ref.shape[0]
    kv_count = k_ref.shape[1] // HD
    group = q_ref.shape[1] // k_ref.shape[1]
    width = group * HD
    sections = plan_ref.shape[1]
    spread = peers // line_size
    slot_rows = line_size * sections * TILE
    remote_rows = spread * slot_rows
    factor = 1.0 / math.sqrt(HD)
    me = lax.axis_index("ctx")
    place = me // spread
    lane_id = lax.rem(me, spread)
    head_id = lax.axis_index("head")

    def partner(offset):
        return lax.rem(lane_id + offset, spread)

    barrier = pltpu.get_barrier_semaphore()

    def greet(offset, carry):
        pl.semaphore_signal(barrier, inc=1, device_id={"ctx": place * spread + partner(offset)})
        return carry

    lax.fori_loop(1, spread, greet, 0)
    for offset in range(1, head_peers):
        pl.semaphore_signal(
            barrier, inc=1, device_id={"head": lax.rem(head_id + offset, head_peers)}
        )
    if line_size > 1:
        @pl.when(place > 0)
        def _():
            pl.semaphore_signal(barrier, inc=1, device_id={"ctx": me - spread})

        @pl.when(place < line_size - 1)
        def _():
            pl.semaphore_signal(barrier, inc=1, device_id={"ctx": me + spread})

    def columns(plan_rows, which):
        row = lax.broadcasted_iota(jnp.int32, (slot_rows, peers), 0)
        lane = lax.broadcasted_iota(jnp.int32, (slot_rows, peers), 1)
        hit = lane == (row // (sections * TILE)) * spread + which
        section = (row // TILE) % sections
        total = jnp.zeros((slot_rows, peers), jnp.float32)
        for index in range(sections):
            total = total + jnp.where(
                hit & (section == index), plan_rows[index : index + 1, :], 0.0
            )
        return jnp.sum(total, axis=1, keepdims=True)

    def build_pick(which, carry):
        plan_rows = plan_ref[place * spread + which].astype(jnp.float32)
        tile = columns(plan_rows, lane_id).astype(jnp.int32)
        shape = (slot_rows, line_size * rows)
        row = lax.broadcasted_iota(jnp.int32, shape, 0)
        lane = lax.broadcasted_iota(jnp.int32, shape, 1)
        target = (row // (sections * TILE)) * rows + tile * TILE + row % TILE
        pick[which] = jnp.where((tile >= 0) & (lane == target), 1.0, 0.0).astype(jnp.bfloat16)
        return carry

    lax.fori_loop(0, spread, build_pick, 0)

    def fill(head, carry):
        at = pl.ds(pl.multiple_of(head * HD, HD), HD)
        line[head, place] = jnp.concatenate([k_ref[:, at], v_ref[:, at]], axis=1)
        return carry

    lax.fori_loop(0, kv_count, fill, 0)

    waits = spread - 1 + head_peers - 1
    if waits > 0:
        pl.semaphore_wait(barrier, waits)
    if line_size > 1:
        @pl.when(place > 0)
        def _():
            pl.semaphore_wait(barrier, 1)

        @pl.when(place < line_size - 1)
        def _():
            pl.semaphore_wait(barrier, 1)

    def hop(head, way, step, origin):
        return pltpu.make_async_remote_copy(
            src_ref=line.at[head, origin],
            dst_ref=line.at[head, origin],
            send_sem=l_send.at[head, way, step],
            recv_sem=l_recv.at[head, way, step],
            device_id={"ctx": me + (spread if way == 0 else -spread)},
        )

    def hop_start(head, step):
        @pl.when((place >= step) & (place < line_size - 1))
        def _():
            hop(head, 0, step, place - step).start()

        @pl.when((place + step <= line_size - 1) & (place > 0))
        def _():
            hop(head, 1, step, place + step).start()

    def hop_wait(head, step):
        @pl.when(place - 1 - step >= 0)
        def _():
            hop(head, 0, step, place - 1 - step).wait_recv()

        @pl.when(place + 1 + step <= line_size - 1)
        def _():
            hop(head, 1, step, place + 1 + step).wait_recv()

    def hop_sent(head, step):
        @pl.when((place >= step) & (place < line_size - 1))
        def _():
            hop(head, 0, step, place - step).wait_send()

        @pl.when((place + step <= line_size - 1) & (place > 0))
        def _():
            hop(head, 1, step, place + step).wait_send()

    def exchange(source, target, send, recv, head, offset, slot):
        return pltpu.make_async_remote_copy(
            src_ref=source.at[head, partner(offset)],
            dst_ref=target.at[head, slot],
            send_sem=send.at[head, offset],
            recv_sem=recv.at[head, offset],
            device_id={"ctx": place * spread + partner(offset)},
        )

    def each(body):
        def step(offset, carry):
            body(offset)
            return carry

        lax.fori_loop(1, spread, step, 0)

    def front(head):
        for step in range(line_size - 1):
            hop_wait(head, step)
            if step + 1 < line_size - 1:
                hop_start(head, step + 1)
        flat = pick[...].reshape(remote_rows, line_size * rows)
        chosen = contract(flat, line[head].reshape(line_size * rows, 2 * HD), 1, 0)
        x_out[head] = chosen.astype(jnp.bfloat16).reshape(spread, slot_rows, 2 * HD)
        each(lambda o: exchange(x_out, x_in, x_send, x_recv, head, o, lane_id).start())
        x_in[head, lane_id] = x_out[head, lane_id]

    gate_row = jax.nn.sigmoid(gate_row_ref[...])
    gate_col = jax.nn.sigmoid(gate_col_ref[...])

    def prepare(head):
        for index in range(group):
            at = pl.ds(pl.multiple_of(head * width + index * HD, HD), HD)
            here = slice(index * HD, (index + 1) * HD)
            query = q_ref[:, at]
            grad = og_ref[:, at].astype(jnp.float32)
            grad_col = grad.T
            q_rows[head, here, :] = query
            q_cols[head, :, here] = query.astype(jnp.float32).T.astype(jnp.bfloat16)
            og_cols[head, :, here] = grad_col.astype(jnp.bfloat16)
            da_rows[head, here, :] = (gate_col * grad).astype(jnp.bfloat16)
            da_cols[head, :, here] = (gate_row * grad_col).astype(jnp.bfloat16)

    def build_bias():
        late = (
            lax.broadcasted_iota(jnp.int32, (slot_rows, rows), 1) >= rows // 2
        ).astype(jnp.float32)
        own_row = lax.broadcasted_iota(jnp.int32, (rows, rows), 0)
        own_lane = lax.broadcasted_iota(jnp.int32, (rows, rows), 1)
        bias[0:rows, :] = jnp.where(own_row <= own_lane, 0.0, NEG)
        seen = jnp.where(
            plan_ref[me] >= 0, 2.0 - kind_ref[0].astype(jnp.float32), 0.0
        )
        for which in range(spread):
            code = columns(seen, which)
            start = rows + which * slot_rows
            bias[start : start + slot_rows, :] = jnp.where(code + late >= 2.0, 0.0, NEG)

    pair = 2 if group % 2 == 0 else 1
    pair_width = pair * HD

    def middle(head):
        each(
            lambda o: exchange(
                x_out, x_in, x_send, x_recv, head, o, partner(spread - o)
            ).wait_recv()
        )
        kv_all[0:rows, :] = line[head, place]
        kv_all[rows:, :] = x_in[head].reshape(remote_rows, 2 * HD)
        keys = kv_all[:, 0:HD]
        values = kv_all[:, HD:]
        mask = jnp.concatenate([bias[...]] * pair, axis=1)
        for index in range(group // pair):
            here = slice(index * pair_width, (index + 1) * pair_width)
            scores = contract(keys, q_cols[head, :, here], 1, 0)
            scores = scores * (factor * math.log2(math.e)) + mask
            top = jnp.max(scores, axis=0, keepdims=True)
            probs = jnp.exp2(scores - top)
            probs = probs * (1.0 / jnp.sum(probs, axis=0, keepdims=True))
            probs_low = probs.astype(jnp.bfloat16)
            probs_kept[:, here] = probs_low
            attended = contract(values, probs_low, 0, 0)
            attended = attended.astype(jnp.bfloat16).astype(jnp.float32)
            da_here = da_cols[head, :, here]
            delta = jnp.sum(da_here.astype(jnp.float32) * attended, axis=0, keepdims=True)
            gate_term = jnp.sum(
                og_cols[head, :, here].astype(jnp.float32) * attended, axis=0, keepdims=True
            )
            for part in range(pair):
                term = gate_term[:, part * HD : (part + 1) * HD]
                gate_parts[head_id] += jnp.broadcast_to(term, (8, HD))
            d_probs = contract(values, da_here, 1, 0)
            scores_kept[head, :, here] = (probs * (d_probs - delta)).astype(jnp.bfloat16)
        d_values = contract(probs_kept[...], da_rows[head], 1, 0)
        d_keys = contract(scores_kept[head], q_rows[head], 1, 0) * factor
        both = jnp.concatenate([d_keys, d_values], axis=1)
        own_grad[head] = both[0:rows]
        g_out[head] = both[rows:].astype(jnp.bfloat16).reshape(spread, slot_rows, 2 * HD)
        each(lambda o: exchange(g_out, g_in, g_send, g_recv, head, o, lane_id).start())
        g_in[head, lane_id] = g_out[head, lane_id]
        kept_keys = kv_all[:, 0:HD]
        d_queries = contract(kept_keys, scores_kept[head], 0, 0) * factor
        for index in range(group):
            at = pl.ds(pl.multiple_of(head * width + index * HD, HD), HD)
            dq_ref[:, at] = d_queries[:, index * HD : (index + 1) * HD].T.astype(jnp.bfloat16)

    def chain(head, way, step):
        return pltpu.make_async_remote_copy(
            src_ref=r_send_buf.at[head, way, step],
            dst_ref=r_recv_buf.at[head, way, step],
            send_sem=r_send.at[head, way, step],
            recv_sem=r_recv.at[head, way, step],
            device_id={"ctx": me + (spread if way == 0 else -spread)},
        )

    def chain_roles(way, step):
        if way == 0:
            owner = line_size - 1 - step
            return owner, place < owner, place == 0
        owner = step
        return owner, place > owner, place == line_size - 1

    def back(head):
        each(
            lambda o: exchange(
                g_out, g_in, g_send, g_recv, head, o, partner(spread - o)
            ).wait_recv()
        )
        flat = pick[...].reshape(remote_rows, line_size * rows)
        dense = contract(flat, g_in[head].reshape(remote_rows, 2 * HD), 0, 0)
        if line_size > 1:
            for step in range(line_size - 1):
                for way in range(2):
                    owner, passes, first = chain_roles(way, step)
                    mine = dense[owner * rows : (owner + 1) * rows]

                    @pl.when(passes & first)
                    def _():
                        r_send_buf[head, way, step] = mine.astype(jnp.bfloat16)
                        chain(head, way, step).start()

                    @pl.when(passes & jnp.logical_not(first))
                    def _():
                        chain(head, way, step).wait_recv()
                        r_send_buf[head, way, step] = (
                            mine + r_recv_buf[head, way, step].astype(jnp.float32)
                        ).astype(jnp.bfloat16)
                        chain(head, way, step).start()

                    @pl.when(place == owner)
                    def _():
                        chain(head, way, step).wait_recv()
                        own_grad[head] += r_recv_buf[head, way, step].astype(jnp.float32)
            for owner in range(line_size):
                @pl.when(place == owner)
                def _():
                    own_grad[head] += dense[owner * rows : (owner + 1) * rows]
        else:
            own_grad[head] += dense
        at = pl.ds(pl.multiple_of(head * HD, HD), HD)
        dk_ref[:, at] = own_grad[head, :, 0:HD].astype(jnp.bfloat16)
        dv_ref[:, at] = own_grad[head, :, HD:].astype(jnp.bfloat16)

    gate_parts[head_id] = jnp.zeros((8, HD), jnp.float32)
    if line_size > 1:
        def begin(head, carry):
            hop_start(head, 0)
            return carry

        lax.fori_loop(0, kv_count, begin, 0)
    else:
        def begin(head, carry):
            front(head)
            return carry

        lax.fori_loop(0, kv_count, begin, 0)

    build_bias()

    def get_ready(head, carry):
        prepare(head)
        return carry

    lax.fori_loop(0, kv_count, get_ready, 0)

    def turn(step, carry):
        if line_size > 1:
            @pl.when(step < kv_count)
            def _():
                front(step)

        @pl.when((step >= 1) & (step <= kv_count))
        def _():
            middle(step - 1)

        @pl.when(step >= 2)
        def _():
            back(step - 2)

        return carry

    lax.fori_loop(0, kv_count + 1, turn, 0)

    def gate_copy(offset, slot):
        return pltpu.make_async_remote_copy(
            src_ref=gate_parts.at[head_id],
            dst_ref=gate_parts.at[slot],
            send_sem=p_send.at[offset],
            recv_sem=p_recv.at[offset],
            device_id={"head": lax.rem(head_id + offset, head_peers)},
        )

    for offset in range(1, head_peers):
        gate_copy(offset, head_id).start()
    back(kv_count - 1)
    for offset in range(1, head_peers):
        gate_copy(offset, lax.rem(head_id + head_peers - offset, head_peers)).wait_recv()
    total = jnp.sum(gate_parts[...], axis=0)
    dgate_ref[...] = gate_row * (1.0 - gate_row) * total[0:1, :]

    for offset in range(1, head_peers):
        gate_copy(offset, head_id).wait_send()

    def finish(head, carry):
        each(lambda o: exchange(x_out, x_in, x_send, x_recv, head, o, lane_id).wait_send())
        each(lambda o: exchange(g_out, g_in, g_send, g_recv, head, o, lane_id).wait_send())
        for step in range(line_size - 1):
            hop_sent(head, step)
            for way in range(2):
                _, passes, _ = chain_roles(way, step)

                @pl.when(passes)
                def _():
                    chain(head, way, step).wait_send()

        return carry

    lax.fori_loop(0, kv_count, finish, 0)


def solution(mesh):
    peers = mesh.shape["ctx"]
    head_peers = mesh.shape["head"]
    line_size = 1
    if LINE:
        while (line_size + 1) ** 2 <= peers:
            line_size += 1
        while peers % line_size:
            line_size -= 1
    spread = peers // line_size

    def body(queries, key_rows, value_rows, out_grad, gate_logit, tile_plan, mask_kind):
        rows = queries.shape[0]
        kv_count = key_rows.shape[1] // HD
        width = queries.shape[1] // kv_count
        sections = tile_plan.shape[1]
        slot_rows = line_size * sections * TILE
        key_count = rows + spread * slot_rows
        hops = max(line_size - 1, 1)
        low, full = jnp.bfloat16, jnp.float32
        vmem = pl.BlockSpec(memory_space=pltpu.VMEM)
        dma = pltpu.SemaphoreType.DMA
        outs = pl.pallas_call(
            functools.partial(kernel, peers, line_size, head_peers),
            out_shape=(
                jax.ShapeDtypeStruct(queries.shape, low),
                jax.ShapeDtypeStruct(key_rows.shape, low),
                jax.ShapeDtypeStruct(value_rows.shape, low),
                jax.ShapeDtypeStruct((1, rows), full),
            ),
            in_specs=[vmem] * 8,
            out_specs=(vmem,) * 4,
            scratch_shapes=[
                pltpu.VMEM((spread, slot_rows, line_size * rows), low),
                pltpu.VMEM((key_count, rows), full),
                pltpu.VMEM((kv_count, line_size, rows, 2 * HD), low),
                pltpu.VMEM((kv_count, spread, slot_rows, 2 * HD), low),
                pltpu.VMEM((kv_count, spread, slot_rows, 2 * HD), low),
                pltpu.VMEM((kv_count, spread, slot_rows, 2 * HD), low),
                pltpu.VMEM((kv_count, spread, slot_rows, 2 * HD), low),
                pltpu.VMEM((kv_count, rows, 2 * HD), full),
                pltpu.VMEM((kv_count, width, HD), low),
                pltpu.VMEM((kv_count, HD, width), low),
                pltpu.VMEM((kv_count, width, HD), low),
                pltpu.VMEM((kv_count, HD, width), low),
                pltpu.VMEM((kv_count, HD, width), low),
                pltpu.VMEM((key_count, 2 * HD), low),
                pltpu.VMEM((key_count, width), low),
                pltpu.VMEM((kv_count, key_count, width), low),
                pltpu.VMEM((head_peers, 8, rows), full),
                pltpu.VMEM((kv_count, 2, hops, rows, 2 * HD), low),
                pltpu.VMEM((kv_count, 2, hops, rows, 2 * HD), low),
                dma((kv_count, spread)),
                dma((kv_count, spread)),
                dma((kv_count, spread)),
                dma((kv_count, spread)),
                dma((kv_count, 2, hops)),
                dma((kv_count, 2, hops)),
                dma((kv_count, 2, hops)),
                dma((kv_count, 2, hops)),
                dma((head_peers,)),
                dma((head_peers,)),
            ],
            compiler_params=pltpu.CompilerParams(
                collective_id=0, has_side_effects=True, vmem_limit_bytes=56 * 1024 * 1024
            ),
            name="attention_grad",
        )(
            queries,
            key_rows,
            value_rows,
            out_grad,
            gate_logit.reshape(1, rows),
            gate_logit.reshape(rows, 1),
            tile_plan,
            mask_kind,
        )
        return outs[0], outs[1], outs[2], outs[3].reshape(rows)

    return jax.shard_map(
        body,
        mesh=mesh,
        in_specs=(
            P("ctx", "head"),
            P("ctx", "head"),
            P("ctx", "head"),
            P("ctx", "head"),
            P("ctx"),
            P(),
            P("ctx", None, None),
        ),
        out_specs=(P("ctx", "head"), P("ctx", "head"), P("ctx", "head"), P("ctx")),
        check_vma=False,
    )
```

time: 139 us -> 64.8 us (0.47)
  the two profiles are of different devices: /device:TPU:0 before, /device:TPU:1 now
where the time goes in v1:
time: 64.8 us; the launch traced here: 64.6 us
  Pallas kernels  58.3 us (90%)
  local copies, waits for them, and re-layouts  5.62 us (9%)
  between operations  0.66 us (1%)
    pallas_call x1, Pallas kernels, body(): pl.pallas_call(functools.partial(kernel, peers, line_size, head_peers), o...  58.3 us
    unnamed x12, local copies, waits for them, and re-layouts  4.88 us

profile of v1, /device:TPU:1, one launch (start us, length us, event | category | flops | bytes accessed | tf_op | source)
XLA Modules:
  0.0 64.6 jit_solution(4627906664605375262)
XLA Ops:
  0.6 0.0 copy-start.2
  0.6 0.6 %copy-done.2 = f32[128]{0:T(128)S(1)} copy-done((f32[128]{0:T(128)S(1)}, f32[128]{0:T(128)}, u32[]{:S(2)}) %copy-start.2) | copy-done | bytes 536
  1.3 0.7 %copy.11.gate_col_ref = f32[128,1]{1,0:T(8,128)} copy(f32[128,1]{0,1:T(1,128)S(1)} %bitcast.4) | data formatting | bytes 1024 | tf_op jit(solution)/shard_map/reshape | solution.py:499
  2.0 58.3 %attention_grad.1 = (bf16[128,3072]{1,0:T(8,128)(2,1)}, bf16[128,512]{1,0:T(8,128)(2,1)}, bf16[128,512]{1,0:T(8,128)(2,1)}, f32[1,128]{1,0:T(1,128)}) custom-call(bf16[128,3072]{1,0:T(8,128)(2,1)} %q_ref.1, bf16[128,512]{1,0:T(8,128)(2,1)} %k_ref.1, bf16[128,512]{1,0:T(8,128)(2,1)} %v_ref.1, bf16[128,3072]{1,0:T(8,128)(2,1)} %og_ref.1, f32[1,128]{1,0:T(1,128)} %bitcast.3, ...), custom_call_target="tpu_custom_call" | custom-call | tf_op jit(solution)/shard_map/attention_grad/pallas_call | solution.py:448
  60.3 0.0 copy-start.1
  60.3 2.1 %copy.16 = bf16[128,3072]{1,0:T(8,128)(2,1)} copy(bf16[128,3072]{1,0:T(8,128)(2,1)} %get-tuple-element.16) | data formatting | bytes 1572864
  62.4 0.0 copy-done.1
  62.4 0.0 copy-start
  62.4 0.7 %copy.17 = bf16[128,512]{1,0:T(8,128)(2,1)} copy(bf16[128,512]{1,0:T(8,128)(2,1)S(1)} %copy-done.1) | data formatting | bytes 262144
  63.1 0.3 copy-done
  63.4 0.0 copy-start.3
  63.4 0.7 %copy.18 = bf16[128,512]{1,0:T(8,128)(2,1)} copy(bf16[128,512]{1,0:T(8,128)(2,1)S(1)} %copy-done) | data formatting | bytes 262144
  64.0 0.0 copy-done.3
  64.0 0.5 copy.19
Async XLA Ops:
  0.6 0.7 %copy-start.2 = (f32[128]{0:T(128)S(1)}, f32[128]{0:T(128)}, u32[]{:S(2)}) copy-start(f32[128]{0:T(128)} %param.11) | copy-start | bytes 1540
  60.3 2.1 %copy-start.1 = (bf16[128,512]{1,0:T(8,128)(2,1)S(1)}, bf16[128,512]{1,0:T(8,128)(2,1)}, u32[]{:S(2)}) copy-start(bf16[128,512]{1,0:T(8,128)(2,1)} %get-tuple-element.17) | copy-start | bytes 393220
  62.4 1.0 %copy-start = (bf16[128,512]{1,0:T(8,128)(2,1)S(1)}, bf16[128,512]{1,0:T(8,128)(2,1)}, u32[]{:S(2)}) copy-start(bf16[128,512]{1,0:T(8,128)(2,1)} %get-tuple-element.18) | copy-start | bytes 393220
  63.4 0.7 %copy-start.3 = (f32[1,128]{1,0:T(1,128)S(1)}, f32[1,128]{1,0:T(1,128)}, u32[]{:S(2)}) copy-start(f32[1,128]{1,0:T(1,128)} %get-tuple-element.11) | copy-start | bytes 1540

commit v2 on v1

--- a/solution.py
+++ b/solution.py
@@ -10,7 +10,7 @@
 
 HD = 128
 TILE = 8
-LINE = False
+LINE = True
 
 NEG = -1e30
 
@@ -135,17 +135,9 @@
 
     lax.fori_loop(0, kv_count, fill, 0)
 
-    waits = spread - 1 + head_peers - 1
-    if waits > 0:
-        pl.semaphore_wait(barrier, waits)
-    if line_size > 1:
-        @pl.when(place > 0)
-        def _():
-            pl.semaphore_wait(barrier, 1)
-
-        @pl.when(place < line_size - 1)
-        def _():
-            pl.semaphore_wait(barrier, 1)
+    below = (place + line_size - 1) // line_size
+    above = (2 * (line_size - 1) - place) // line_size
+    pl.semaphore_wait(barrier, spread - 1 + head_peers - 1 + below + above)
 
     def hop(head, way, step, origin):
         return pltpu.make_async_remote_copy(

time: 64.8 us -> 162 us (2.50)
  the two profiles are of different devices: /device:TPU:1 before, /device:TPU:10 now
where the time goes in v2:
time: 162 us
  Pallas kernels  156 us (96%)
  local copies, waits for them, and re-layouts  5.62 us (3%)
    pallas_call x1, Pallas kernels, body(): pl.pallas_call(functools.partial(kernel, peers, line_size, head_peers), o...  156 us
    unnamed x12, local copies, waits for them, and re-layouts  4.88 us

profile of v2, /device:TPU:10, one launch (start us, length us, event | category | flops | bytes accessed | tf_op | source)
XLA Modules:
  0.0 162.2 jit_solution(5944883312563733021)
XLA Ops:
  0.6 0.0 copy-start.2
  0.6 0.6 copy-done.2
  1.3 0.7 copy.11.gate_col_ref
  2.0 155.9 %attention_grad.1 = (bf16[128,3072]{1,0:T(8,128)(2,1)}, bf16[128,512]{1,0:T(8,128)(2,1)}, bf16[128,512]{1,0:T(8,128)(2,1)}, f32[1,128]{1,0:T(1,128)}) custom-call(bf16[128,3072]{1,0:T(8,128)(2,1)} %q_ref.1, bf16[128,512]{1,0:T(8,128)(2,1)} %k_ref.1, bf16[128,512]{1,0:T(8,128)(2,1)} %v_ref.1, bf16[128,3072]{1,0:T(8,128)(2,1)} %og_ref.1, f32[1,128]{1,0:T(1,128)} %bitcast.3, ...), custom_call_target="tpu_custom_call" | custom-call | tf_op jit(solution)/shard_map/attention_grad/pallas_call | solution.py:440
  157.9 0.0 copy-start.1
  157.9 2.1 %copy.16 = bf16[128,3072]{1,0:T(8,128)(2,1)} copy(bf16[128,3072]{1,0:T(8,128)(2,1)} %get-tuple-element.16) | data formatting | bytes 1572864
  160.0 0.0 copy-done.1
  160.0 0.0 copy-start
  160.0 0.7 copy.17
  160.7 0.3 copy-done
  161.0 0.0 copy-start.3
  161.0 0.7 copy.18
  161.6 0.0 copy-done.3
  161.6 0.5 copy.19
Async XLA Ops:
  0.6 0.7 copy-start.2
  157.9 2.1 %copy-start.1 = (bf16[128,512]{1,0:T(8,128)(2,1)S(1)}, bf16[128,512]{1,0:T(8,128)(2,1)}, u32[]{:S(2)}) copy-start(bf16[128,512]{1,0:T(8,128)(2,1)} %get-tuple-element.17) | copy-start | bytes 393220
  160.0 1.0 copy-start
  161.0 0.7 copy-start.3

commit v3 on v2

--- a/solution.py
+++ b/solution.py
@@ -10,7 +10,7 @@
 
 HD = 128
 TILE = 8
-LINE = True
+LINE = 2
 
 NEG = -1e30
 
@@ -30,7 +30,6 @@
     v_ref,
     og_ref,
     gate_row_ref,
-    gate_col_ref,
     plan_ref,
     kind_ref,
     dq_ref,
@@ -203,7 +202,7 @@
         x_in[head, lane_id] = x_out[head, lane_id]
 
     gate_row = jax.nn.sigmoid(gate_row_ref[...])
-    gate_col = jax.nn.sigmoid(gate_col_ref[...])
+    gate_col = jnp.broadcast_to(gate_row, (HD, rows)).T
 
     def prepare(head):
         for index in range(group):
@@ -277,9 +276,7 @@
         g_in[head, lane_id] = g_out[head, lane_id]
         kept_keys = kv_all[:, 0:HD]
         d_queries = contract(kept_keys, scores_kept[head], 0, 0) * factor
-        for index in range(group):
-            at = pl.ds(pl.multiple_of(head * width + index * HD, HD), HD)
-            dq_ref[:, at] = d_queries[:, index * HD : (index + 1) * HD].T.astype(jnp.bfloat16)
+        dq_ref[head] = d_queries.astype(jnp.bfloat16)
 
     def chain(head, way, step):
         return pltpu.make_async_remote_copy(
@@ -415,15 +412,22 @@
     lax.fori_loop(0, kv_count, finish, 0)
 
 
+def write(dq_cols_ref, dk_in_ref, dv_in_ref, dgate_in_ref, dq_ref, dk_ref, dv_ref, dgate_ref):
+    kv_count, _, width = dq_cols_ref.shape
+    for head in range(kv_count):
+        for index in range(width // HD):
+            start = head * width + index * HD
+            part = dq_cols_ref[head, :, index * HD : (index + 1) * HD]
+            dq_ref[:, start : start + HD] = part.T
+    dk_ref[...] = dk_in_ref[...]
+    dv_ref[...] = dv_in_ref[...]
+    dgate_ref[...] = dgate_in_ref[...]
+
+
 def solution(mesh):
     peers = mesh.shape["ctx"]
     head_peers = mesh.shape["head"]
-    line_size = 1
-    if LINE:
-        while (line_size + 1) ** 2 <= peers:
-            line_size += 1
-        while peers % line_size:
-            line_size -= 1
+    line_size = LINE if peers % LINE == 0 else 1
     spread = peers // line_size
 
     def body(queries, key_rows, value_rows, out_grad, gate_logit, tile_plan, mask_kind):
@@ -440,12 +444,12 @@
         outs = pl.pallas_call(
             functools.partial(kernel, peers, line_size, head_peers),
             out_shape=(
-                jax.ShapeDtypeStruct(queries.shape, low),
+                jax.ShapeDtypeStruct((kv_count, HD, width), low),
                 jax.ShapeDtypeStruct(key_rows.shape, low),
                 jax.ShapeDtypeStruct(value_rows.shape, low),
                 jax.ShapeDtypeStruct((1, rows), full),
             ),
-            in_specs=[vmem] * 8,
+            in_specs=[vmem] * 7,
             out_specs=(vmem,) * 4,
             scratch_shapes=[
                 pltpu.VMEM((spread, slot_rows, line_size * rows), low),
@@ -488,10 +492,21 @@
             value_rows,
             out_grad,
             gate_logit.reshape(1, rows),
-            gate_logit.reshape(rows, 1),
             tile_plan,
             mask_kind,
         )
+        outs = pl.pallas_call(
+            write,
+            out_shape=(
+                jax.ShapeDtypeStruct(queries.shape, low),
+                jax.ShapeDtypeStruct(key_rows.shape, low),
+                jax.ShapeDtypeStruct(value_rows.shape, low),
+                jax.ShapeDtypeStruct((1, rows), full),
+            ),
+            in_specs=[vmem] * 4,
+            out_specs=(vmem,) * 4,
+            name="write_grads",
+        )(*outs)
         return outs[0], outs[1], outs[2], outs[3].reshape(rows)
 
     return jax.shard_map(

time: 162 us -> 77.9 us (0.48)
  the two profiles are of different devices: /device:TPU:10 before, /device:TPU:0 now
where the time goes in v3:
time: 77.9 us; the launch traced here: 77.8 us
  Pallas kernels  77.1 us (99%)
    pallas_call x1, Pallas kernels, body(): pl.pallas_call(functools.partial(kernel, peers, line_size, head_peers), o...  74.7 us
    pallas_call x1, Pallas kernels, body(): pl.pallas_call(write, out_shape=(jax.ShapeDtypeStruct(queries.shape, low)...  2.38 us

profile of v3, /device:TPU:0, one launch (start us, length us, event | category | flops | bytes accessed | tf_op | source)
XLA Modules:
  0.0 77.8 jit_solution(14393866639904928868)
XLA Ops:
  0.6 74.7 %attention_grad.1 = (bf16[4,128,768]{2,1,0:T(8,128)(2,1)}, bf16[128,512]{1,0:T(8,128)(2,1)}, bf16[128,512]{1,0:T(8,128)(2,1)}, f32[1,128]{1,0:T(1,128)}) custom-call(bf16[128,3072]{1,0:T(8,128)(2,1)} %q_ref.1, bf16[128,512]{1,0:T(8,128)(2,1)} %k_ref.1, bf16[128,512]{1,0:T(8,128)(2,1)} %v_ref.1, bf16[128,3072]{1,0:T(8,128)(2,1)} %og_ref.1, f32[1,128]{1,0:T(1,128)} %bitcast.2, ...), custom_call_target="tpu_custom_call" | custom-call | tf_op jit(solution)/shard_map/attention_grad/pallas_call | solution.py:444
  75.4 2.4 %write_grads.1 = (bf16[128,3072]{1,0:T(8,128)(2,1)}, bf16[128,512]{1,0:T(8,128)(2,1)}, bf16[128,512]{1,0:T(8,128)(2,1)}, f32[1,128]{1,0:T(1,128)}) custom-call(bf16[4,128,768]{2,1,0:T(8,128)(2,1)} %get-tuple-element.12.dq_cols_ref, bf16[128,512]{1,0:T(8,128)(2,1)} %get-tuple-element.13.dk_in_ref, bf16[128,512]{1,0:T(8,128)(2,1)} %get-tuple-element.14.dv_in_ref, ...), custom_call_target="tpu_custom_call" | custom-call | tf_op jit(solution)/shard_map/write_grads/pallas_call | solution.py:498

commit v4 on v3

--- a/solution.py
+++ b/solution.py
@@ -10,7 +10,7 @@
 
 HD = 128
 TILE = 8
-LINE = 2
+LINE = 1
 
 NEG = -1e30
 
@@ -241,10 +241,10 @@
                 x_out, x_in, x_send, x_recv, head, o, partner(spread - o)
             ).wait_recv()
         )
-        kv_all[0:rows, :] = line[head, place]
-        kv_all[rows:, :] = x_in[head].reshape(remote_rows, 2 * HD)
-        keys = kv_all[:, 0:HD]
-        values = kv_all[:, HD:]
+        kv_all[head, 0:rows, :] = line[head, place]
+        kv_all[head, rows:, :] = x_in[head].reshape(remote_rows, 2 * HD)
+        keys = kv_all[head, :, 0:HD]
+        values = kv_all[head, :, HD:]
         mask = jnp.concatenate([bias[...]] * pair, axis=1)
         for index in range(group // pair):
             here = slice(index * pair_width, (index + 1) * pair_width)
@@ -274,9 +274,12 @@
         g_out[head] = both[rows:].astype(jnp.bfloat16).reshape(spread, slot_rows, 2 * HD)
         each(lambda o: exchange(g_out, g_in, g_send, g_recv, head, o, lane_id).start())
         g_in[head, lane_id] = g_out[head, lane_id]
-        kept_keys = kv_all[:, 0:HD]
-        d_queries = contract(kept_keys, scores_kept[head], 0, 0) * factor
-        dq_ref[head] = d_queries.astype(jnp.bfloat16)
+
+    def queries_grad(head):
+        d_queries = contract(kv_all[head, :, 0:HD], scores_kept[head], 0, 0) * factor
+        for index in range(group):
+            at = pl.ds(pl.multiple_of(head * width + index * HD, HD), HD)
+            dq_ref[:, at] = d_queries[:, index * HD : (index + 1) * HD].T.astype(jnp.bfloat16)
 
     def chain(head, way, step):
         return pltpu.make_async_remote_copy(
@@ -363,13 +366,9 @@
             def _():
                 front(step)
 
-        @pl.when((step >= 1) & (step <= kv_count))
+        @pl.when(step >= 1)
         def _():
             middle(step - 1)
-
-        @pl.when(step >= 2)
-        def _():
-            back(step - 2)
 
         return carry
 
@@ -386,7 +385,17 @@
 
     for offset in range(1, head_peers):
         gate_copy(offset, head_id).start()
-    back(kv_count - 1)
+
+    def queries_turn(head, carry):
+        queries_grad(head)
+        return carry
+
+    def back_turn(head, carry):
+        back(head)
+        return carry
+
+    lax.fori_loop(0, kv_count, queries_turn, 0)
+    lax.fori_loop(0, kv_count, back_turn, 0)
     for offset in range(1, head_peers):
         gate_copy(offset, lax.rem(head_id + head_peers - offset, head_peers)).wait_recv()
     total = jnp.sum(gate_parts[...], axis=0)
@@ -412,13 +421,8 @@
     lax.fori_loop(0, kv_count, finish, 0)
 
 
-def write(dq_cols_ref, dk_in_ref, dv_in_ref, dgate_in_ref, dq_ref, dk_ref, dv_ref, dgate_ref):
-    kv_count, _, width = dq_cols_ref.shape
-    for head in range(kv_count):
-        for index in range(width // HD):
-            start = head * width + index * HD
-            part = dq_cols_ref[head, :, index * HD : (index + 1) * HD]
-            dq_ref[:, start : start + HD] = part.T
+def write(dq_in_ref, dk_in_ref, dv_in_ref, dgate_in_ref, dq_ref, dk_ref, dv_ref, dgate_ref):
+    dq_ref[...] = dq_in_ref[...]
     dk_ref[...] = dk_in_ref[...]
     dv_ref[...] = dv_in_ref[...]
     dgate_ref[...] = dgate_in_ref[...]
@@ -444,7 +448,7 @@
         outs = pl.pallas_call(
             functools.partial(kernel, peers, line_size, head_peers),
             out_shape=(
-                jax.ShapeDtypeStruct((kv_count, HD, width), low),
+                jax.ShapeDtypeStruct(queries.shape, low),
                 jax.ShapeDtypeStruct(key_rows.shape, low),
                 jax.ShapeDtypeStruct(value_rows.shape, low),
                 jax.ShapeDtypeStruct((1, rows), full),
@@ -465,7 +469,7 @@
                 pltpu.VMEM((kv_count, width, HD), low),
                 pltpu.VMEM((kv_count, HD, width), low),
                 pltpu.VMEM((kv_count, HD, width), low),
-                pltpu.VMEM((key_count, 2 * HD), low),
+                pltpu.VMEM((kv_count, key_count, 2 * HD), low),
                 pltpu.VMEM((key_count, width), low),
                 pltpu.VMEM((kv_count, key_count, width), low),
                 pltpu.VMEM((head_peers, 8, rows), full),

time: 77.9 us -> 60.4 us (0.78)
  Pallas kernels: 77.1 us -> 59.5 us
    pallas_call x1, Pallas kernels: 74.7 us -> 57.4 us  [body(): pl.pallas_call(functools.partial(kernel, peers, line_size, head_peers), o...]
where the time goes in v4:
time: 60.4 us; the launch traced here: 60.2 us
  Pallas kernels  59.5 us (99%)
  between operations  0.64 us (1%)
    pallas_call x1, Pallas kernels, body(): pl.pallas_call(functools.partial(kernel, peers, line_size, head_peers), o...  57.4 us
    pallas_call x1, Pallas kernels, body(): pl.pallas_call(write, out_shape=(jax.ShapeDtypeStruct(queries.shape, low)...  2.19 us

profile of v4, /device:TPU:0, one launch (start us, length us, event | category | flops | bytes accessed | tf_op | source)
XLA Modules:
  0.0 60.2 jit_solution(4541810436364909718)
XLA Ops:
  0.6 57.4 %attention_grad.1 = (bf16[128,3072]{1,0:T(8,128)(2,1)}, bf16[128,512]{1,0:T(8,128)(2,1)}, bf16[128,512]{1,0:T(8,128)(2,1)}, f32[1,128]{1,0:T(1,128)}) custom-call(bf16[128,3072]{1,0:T(8,128)(2,1)} %q_ref.1, bf16[128,512]{1,0:T(8,128)(2,1)} %k_ref.1, bf16[128,512]{1,0:T(8,128)(2,1)} %v_ref.1, bf16[128,3072]{1,0:T(8,128)(2,1)} %og_ref.1, f32[1,128]{1,0:T(1,128)} %bitcast.2, ...), custom_call_target="tpu_custom_call" | custom-call | tf_op jit(solution)/shard_map/attention_grad/pallas_call | solution.py:448
  58.0 2.2 %write_grads.1 = (bf16[128,3072]{1,0:T(8,128)(2,1)}, bf16[128,512]{1,0:T(8,128)(2,1)}, bf16[128,512]{1,0:T(8,128)(2,1)}, f32[1,128]{1,0:T(1,128)}) custom-call(bf16[128,3072]{1,0:T(8,128)(2,1)} %get-tuple-element.12.dq_in_ref, bf16[128,512]{1,0:T(8,128)(2,1)} %get-tuple-element.13.dk_in_ref, bf16[128,512]{1,0:T(8,128)(2,1)} %get-tuple-element.14.dv_in_ref, ...), custom_call_target="tpu_custom_call" | custom-call | tf_op jit(solution)/shard_map/write_grads/pallas_call | solution.py:502

commit v5 on v4

--- a/solution.py
+++ b/solution.py
@@ -184,8 +184,8 @@
         )
 
     def each(body):
-        def step(offset, carry):
-            body(offset)
+        def step(turn, carry):
+            body(spread // 2 + (turn // 2) * (1 - 2 * lax.rem(turn, 2)))
             return carry
 
         lax.fori_loop(1, spread, step, 0)

time: 60.4 us -> 62.5 us (1.035)
  Pallas kernels: 59.5 us -> 61.7 us
    pallas_call x1, Pallas kernels: 57.4 us -> 59.5 us  [body(): pl.pallas_call(functools.partial(kernel, peers, line_size, head_peers), o...]
where the time goes in v5:
time: 62.5 us; the launch traced here: 62.4 us
  Pallas kernels  61.7 us (99%)
  between operations  0.64 us (1%)
    pallas_call x1, Pallas kernels, body(): pl.pallas_call(functools.partial(kernel, peers, line_size, head_peers), o...  59.5 us
    pallas_call x1, Pallas kernels, body(): pl.pallas_call(write, out_shape=(jax.ShapeDtypeStruct(queries.shape, low)...  2.19 us

profile of v5, /device:TPU:0, one launch (start us, length us, event | category | flops | bytes accessed | tf_op | source)
XLA Modules:
  0.0 62.4 jit_solution(13804547855464926611)
XLA Ops:
  0.6 59.5 %attention_grad.1 = (bf16[128,3072]{1,0:T(8,128)(2,1)}, bf16[128,512]{1,0:T(8,128)(2,1)}, bf16[128,512]{1,0:T(8,128)(2,1)}, f32[1,128]{1,0:T(1,128)}) custom-call(bf16[128,3072]{1,0:T(8,128)(2,1)} %q_ref.1, bf16[128,512]{1,0:T(8,128)(2,1)} %k_ref.1, bf16[128,512]{1,0:T(8,128)(2,1)} %v_ref.1, bf16[128,3072]{1,0:T(8,128)(2,1)} %og_ref.1, f32[1,128]{1,0:T(1,128)} %bitcast.2, ...), custom_call_target="tpu_custom_call" | custom-call | tf_op jit(solution)/shard_map/attention_grad/pallas_call | solution.py:448
  60.2 2.2 %write_grads.1 = (bf16[128,3072]{1,0:T(8,128)(2,1)}, bf16[128,512]{1,0:T(8,128)(2,1)}, bf16[128,512]{1,0:T(8,128)(2,1)}, f32[1,128]{1,0:T(1,128)}) custom-call(bf16[128,3072]{1,0:T(8,128)(2,1)} %get-tuple-element.12.dq_in_ref, bf16[128,512]{1,0:T(8,128)(2,1)} %get-tuple-element.13.dk_in_ref, bf16[128,512]{1,0:T(8,128)(2,1)} %get-tuple-element.14.dv_in_ref, ...), custom_call_target="tpu_custom_call" | custom-call | tf_op jit(solution)/shard_map/write_grads/pallas_call | solution.py:502
